TPU v7x, 32 devices: a whole 2x2x4 slice. The times are simulated.
32 devices in a mesh: groups: 2 (over y), node: 4 (over z), irrep: 4 (over x, core).
Axes of the slice: x: 2, y: 2, z: 4, core: 2. Of those that a mesh axis runs over, the one named last changes fastest.
Arguments:
- node_feats: bfloat16 [49, 128, 1024], P(None, 'irrep', ('groups', 'node')), parts along dimension 2, may hold values from -6 to 6
- cotangent: bfloat16 [49, 128, 1024], P(None, 'irrep', ('groups', 'node')), parts along dimension 2, may hold values from -6 to 6
- wigner: bfloat16 [235, 8192], P(None, ('groups', 'node')), parts along dimension 1, may hold values from -1.1953125 to 1.1953125
- sources: int32 [8192], P(('groups', 'node')), parts along dimension 0, may hold values from 0 to 511, as said below
- targets: int32 [8192], P(('groups', 'node')), parts along dimension 0, may hold values from 0 to 511, as said below
- counts: int32 [64], P(('groups', 'node')), parts along dimension 0, may hold values from 1 to 128, as said below
- first_zero: bfloat16 [896, 896], replicated, may hold values from -0.1875 to 0.1875
- first_one: bfloat16 [2, 768, 768], replicated, may hold values from -0.15625 to 0.15625
- first_two: bfloat16 [2, 640, 640], replicated, may hold values from -0.15625 to 0.15625
- second_zero: bfloat16 [896, 896], replicated, may hold values from -0.1875 to 0.1875
- second_one: bfloat16 [2, 768, 768], replicated, may hold values from -0.15625 to 0.15625
- second_two: bfloat16 [2, 640, 640], replicated, may hold values from -0.15625 to 0.15625
Outputs:
- node_update: bfloat16 [49, 128, 1024], P(None, 'irrep', ('groups', 'node')), parts along dimension 2
- source_grad: float32 [49, 128, 1024], P(None, 'irrep', ('groups', 'node')), parts along dimension 2
There are 2 independent parts, one for each index of `groups`. A program takes and returns all parts, laid end to end along the dimension named above; an argument that names none is the same for every part. Nothing has to cross between parts.
Inputs may be any that keep to these rules, and one draw needn't show every extreme that they name: `targets`: edge slot e belongs to shard s = e // 1024, and its destination atom lies in s * 128 .. s * 128 + 127. `sources`: of the 1024 edge slots of one shard, at most 512 have source atoms in one node shard's range of 128 atoms, and in every shard that most is reached. Block b's live edges sit in its first counts[b] slots; the other slots hold valid indices and are ignored. The first block of every shard is full, the second holds one live edge.
All inputs are finite; a program needn't handle non-finite values.
Results may differ from a plain program's by a relative error of at most 0.0071.
Values may be sent and summed in bfloat16 or wider, within the bound.
A program may use at most 192 MiB of HBM per device.

v0:
```python
import jax
import jax.numpy as jnp
from jax import lax
from jax.sharding import PartitionSpec as P

LMAX = 6
MMAX = 2


edge_scale = 0.5


def frame_row(degree, order_num):
    top_rows = LMAX + 1
    if order_num == 0:
        return degree
    if order_num == 1:
        return top_rows + degree - 1
    if order_num == -1:
        return top_rows + LMAX + degree - 1
    if order_num == 2:
        return top_rows + 2 * LMAX + degree - 2
    return top_rows + 3 * LMAX - 1 + degree - 2


def rotate_in(values, wigner):
    frame_rows = {}
    offset = 0
    for degree in range(LMAX + 1):
        keep_count = min(degree, MMAX)
        col_count = 2 * degree + 1
        row_total = 2 * keep_count + 1
        rot_block = wigner[offset : offset + row_total * col_count].astype(jnp.float32)
        offset += row_total * col_count
        deg_part = values[degree * degree : degree * degree + col_count].astype(jnp.float32)
        for row_index in range(row_total):
            summed = rot_block[row_index * col_count][None, :] * deg_part[0]
            for col_index in range(1, col_count):
                summed = (
                    summed
                    + rot_block[row_index * col_count + col_index][None, :] * deg_part[col_index]
                )
            frame_rows[frame_row(degree, row_index - keep_count)] = summed
    return jnp.stack([frame_rows[position] for position in range(len(frame_rows))])


def rotate_out(frame, wigner):
    degree_rows = []
    offset = 0
    for degree in range(LMAX + 1):
        keep_count = min(degree, MMAX)
        col_count = 2 * degree + 1
        row_total = 2 * keep_count + 1
        rot_block = wigner[offset : offset + row_total * col_count].astype(jnp.float32)
        offset += row_total * col_count
        frame_list = [
            frame[frame_row(degree, row_index - keep_count)].astype(jnp.float32)
            for row_index in range(row_total)
        ]
        for col_index in range(col_count):
            summed = rot_block[col_index][None, :] * frame_list[0]
            for row_index in range(1, row_total):
                summed = (
                    summed
                    + rot_block[row_index * col_count + col_index][None, :] * frame_list[row_index]
                )
            degree_rows.append(summed)
    return jnp.stack(degree_rows)


def apply_matrix(matrix, operand, transposed):
    if transposed:
        return lax.dot_general(
            matrix, operand, (((0,), (0,)), ((), ())), preferred_element_type=jnp.float32
        )
    return jnp.dot(matrix, operand, preferred_element_type=jnp.float32)


def mix_orders(weights, frame, transposed):
    w_zero, w_one, w_two = weights
    channels = frame.shape[1]
    edge_count = frame.shape[2]
    top_rows = LMAX + 1

    def flatten_rows(row_start, row_stop):
        return frame[row_start:row_stop].reshape((row_stop - row_start) * channels, edge_count)

    zero_out = apply_matrix(w_zero, flatten_rows(0, top_rows), transposed)
    out_list = [zero_out.reshape(top_rows, channels, edge_count)]
    row_start = top_rows
    for order_num in (1, 2):
        matrix = w_one if order_num == 1 else w_two
        order_rows = LMAX + 1 - order_num
        plus_rows = flatten_rows(row_start, row_start + order_rows)
        minus_rows = flatten_rows(row_start + order_rows, row_start + 2 * order_rows)
        if transposed:
            plus_part = apply_matrix(matrix[0], plus_rows, True) + apply_matrix(
                matrix[1], minus_rows, True
            )
            minus_part = apply_matrix(matrix[0], minus_rows, True) - apply_matrix(
                matrix[1], plus_rows, True
            )
        else:
            plus_part = apply_matrix(matrix[0], plus_rows, False) - apply_matrix(
                matrix[1], minus_rows, False
            )
            minus_part = apply_matrix(matrix[1], plus_rows, False) + apply_matrix(
                matrix[0], minus_rows, False
            )
        out_list.append(plus_part.reshape(order_rows, channels, edge_count))
        out_list.append(minus_part.reshape(order_rows, channels, edge_count))
        row_start += 2 * order_rows
    return jnp.concatenate(out_list, axis=0)


def gate_forward(hidden):
    scalar = hidden[0]
    gate_sig = jax.nn.sigmoid(scalar)
    return jnp.concatenate([(scalar * gate_sig)[None], hidden[1:] * gate_sig[None]], axis=0).astype(
        jnp.bfloat16
    )


def gate_backward(incoming, hidden):
    scalar = hidden[0]
    gate_sig = jax.nn.sigmoid(scalar)
    first_row = incoming[0] * gate_sig * (1.0 + scalar * (1.0 - gate_sig)) + gate_sig * (
        1.0 - gate_sig
    ) * jnp.sum(incoming[1:] * hidden[1:], axis=0)
    return jnp.concatenate([first_row[None], incoming[1:] * gate_sig[None]], axis=0).astype(
        jnp.bfloat16
    )


def edge_work(first, second, edge_frame, back_seed):
    hidden = mix_orders(first, edge_frame, False)
    gated = gate_forward(hidden)
    message = mix_orders(second, gated, False).astype(jnp.bfloat16)
    back_gate = mix_orders(second, back_seed, True)
    back_hidden = gate_backward(back_gate, hidden)
    back_frame = mix_orders(first, back_hidden, True).astype(jnp.bfloat16)
    return (message, back_frame)


def segment_add(rows, table):
    coef_count, channels, edge_count = rows.shape
    flat_rows = rows.reshape(coef_count * channels, edge_count)
    summed = jnp.dot(flat_rows, table, preferred_element_type=jnp.float32)
    return summed.reshape(coef_count, channels, table.shape[1])


def local(
    node_feats,
    cotangent,
    wigner,
    sources,
    targets,
    counts,
    first_zero,
    first_one,
    first_two,
    second_zero,
    second_one,
    second_two,
):
    first = (first_zero, first_one, first_two)
    second = (second_zero, second_one, second_two)
    coef_count, channels, atoms_dev = node_feats.shape
    edge_count = sources.shape[0]
    block_count = counts.shape[0]
    block_len = edge_count // block_count
    node_count = lax.axis_size("node")
    node_index = lax.axis_index("node")
    atom_count = atoms_dev * node_count
    live_flag = (jnp.arange(block_len, dtype=jnp.int32)[None, :] < counts[:, None]).reshape(
        edge_count
    )
    live_mask = live_flag.astype(jnp.bfloat16)
    all_nodes = lax.all_gather(node_feats, "node", axis=2, tiled=True)
    source_rows = jnp.take(all_nodes, sources, axis=2)
    local_dst = targets - node_index * atoms_dev
    seed_rows = jnp.take(cotangent, local_dst, axis=2) * live_mask
    row_edges, seed_edges = (
        lax.all_to_all(source_rows, "irrep", split_axis=2, concat_axis=1, tiled=True),
        lax.all_to_all(seed_rows, "irrep", split_axis=2, concat_axis=1, tiled=True),
    )
    share_len = edge_count // lax.axis_size("irrep")
    wig_share = lax.dynamic_slice_in_dim(wigner, lax.axis_index("irrep") * share_len, share_len, 1)
    edge_frame = rotate_in(row_edges, wig_share).astype(jnp.bfloat16)
    back_seed = rotate_in(seed_edges, wig_share).astype(jnp.bfloat16)
    message, back_frame = edge_work(first, second, edge_frame, back_seed)
    sent_edges = rotate_out(message, wig_share).astype(jnp.bfloat16)
    returned_edges = rotate_out(back_frame, wig_share).astype(jnp.bfloat16)
    sent_rows, returned = (
        lax.all_to_all(sent_edges, "irrep", split_axis=1, concat_axis=2, tiled=True),
        lax.all_to_all(returned_edges, "irrep", split_axis=1, concat_axis=2, tiled=True),
    )
    dst_table = (
        (local_dst[:, None] == jnp.arange(atoms_dev, dtype=jnp.int32)[None, :]) & live_flag[:, None]
    ).astype(jnp.bfloat16)
    node_update = (edge_scale * segment_add(sent_rows, dst_table)).astype(jnp.bfloat16)
    src_table = (sources[:, None] == jnp.arange(atom_count, dtype=jnp.int32)[None, :]).astype(
        jnp.bfloat16
    )
    spread = edge_scale * segment_add(returned, src_table)
    source_grad = lax.psum_scatter(spread, "node", scatter_dimension=2, tiled=True)
    return (node_update, source_grad)


def solution(mesh):
    in_specs = (
        P(None, "irrep", ("groups", "node")),
        P(None, "irrep", ("groups", "node")),
        P(None, ("groups", "node")),
        P(("groups", "node")),
        P(("groups", "node")),
        P(("groups", "node")),
        P(),
        P(),
        P(),
        P(),
        P(),
        P(),
    )
    out_specs = (P(None, "irrep", ("groups", "node")), P(None, "irrep", ("groups", "node")))
    return jax.shard_map(local, mesh=mesh, in_specs=in_specs, out_specs=out_specs, check_vma=False)
```

profile of v0, /device:TPU:1, one launch (start us, length us, event | category | flops | bytes accessed | tf_op | source)
XLA Modules:
  0.0 818.3 jit_solution(15837597592695805528)
XLA Ops:
  13.2 9.8 %gather_fusion.1 = bf16[1024,49,32]{1,2,0:T(8,128)(2,1)} fusion(bf16[49,32,128]{0,1,2:T(8,128)(2,1)S(1)} %copy.773, s32[1024]{0:T(1024)S(1)} %fusion.598), kind=kCustom, calls=%fused_computation.1 | custom fusion | bytes 6426624 | tf_op jit(solution)/shard_map/jit(_take)/gather | solution.py:182
  23.0 10.2 %fusion.632 = bf16[1024,32,49]{2,1,0:T(8,128)(2,1)} fusion(bf16[1024]{0:T(1024)(128)(2,1)S(1)} %get-tuple-element.466, bf16[1024,49,32]{1,2,0:T(8,128)(2,1)} %gather_fusion.1, pred[1024]{0:T(1024)(128)(4,1)S(1)} %get-tuple-element.2), kind=kLoop, calls=%fused_computation.1444 | loop fusion | flops 3211264 | bytes 6425600
  33.2 20.1 %reshape.6177 = bf16[4,2,200704]{2,1,0:T(2,128)(2,1)} reshape(bf16[1024,32,49]{2,1,0:T(8,128)(2,1)} %fusion.632) | data formatting | bytes 6422528
  53.3 5.1 all-to-all-start.2
  73.9 21.6 %all-to-all-done.2 = bf16[4,2,200704]{2,1,0:T(2,128)(2,1)} async-done(((bf16[4,2,200704]{2,1,0:T(2,128)(2,1)}), bf16[4,2,200704]{2,1,0:T(2,128)(2,1)}, u32[]{:S(2)}, u32[]{:S(2)}) %all-to-all-start.2) | async-done | bytes 3211296 | tf_op jit(solution)/shard_map/all_to_all | solution.py:185
  95.5 27.2 %reshape.6178 = bf16[1024,32,49]{2,1,0:T(8,128)(2,1)} reshape(bf16[4,2,200704]{2,1,0:T(2,128)(2,1)} %all-to-all-done.2) | data formatting | bytes 6422528
  122.7 13.0 %copy.774 = bf16[49,32,4,256]{3,1,2,0:T(8,128)(2,1)} copy(bf16[49,32,4,256]{0,1,3,2:T(8,128)(2,1)} %bitcast.1675) | data formatting | bytes 6422528 | tf_op jit(solution)/shard_map/all_to_all | solution.py:185
  148.2 8.4 %copy.521 = bf16[49,32,512]{0,1,2:T(8,128)(2,1)} copy(bf16[49,32,512]{2,1,0:T(8,128)(2,1)} %all-gather.2.cloned.1.call-done) | data formatting | bytes 3211264 | tf_op jit(solution)/shard_map/all_gather | solution.py:179
  156.6 12.0 %gather_fusion = bf16[1024,49,32]{1,2,0:T(8,128)(2,1)} fusion(bf16[49,32,512]{0,1,2:T(8,128)(2,1)} %copy.521, s32[1024]{0:T(1024)S(1)} %fusion.597), kind=kCustom, calls=%fused_computation | custom fusion | bytes 6426624 | tf_op jit(solution)/shard_map/jit(_take)/gather | solution.py:180
  168.7 8.7 %fusion.631 = bf16[1024,32,49]{2,1,0:T(8,128)(2,1)} fusion(bf16[1024,49,32]{1,2,0:T(8,128)(2,1)} %gather_fusion, pred[1024]{0:T(1024)(128)(4,1)S(1)} %compare_and_fusion.1), kind=kLoop, calls=%fused_computation.1443 | loop fusion | flops 1605632 | bytes 6423552
  177.4 20.7 %reshape.6175 = bf16[4,2,200704]{2,1,0:T(2,128)(2,1)} reshape(bf16[1024,32,49]{2,1,0:T(8,128)(2,1)} %fusion.631) | data formatting | bytes 6422528
  198.0 5.8 all-to-all-start
  319.3 27.4 %reshape.6176 = bf16[1024,32,49]{2,1,0:T(8,128)(2,1)} reshape(bf16[4,2,200704]{2,1,0:T(2,128)(2,1)} %all-to-all-done) | data formatting | bytes 6422528
  346.7 13.0 %copy.522 = bf16[49,32,4,256]{3,1,2,0:T(8,128)(2,1)} copy(bf16[49,32,4,256]{0,1,3,2:T(8,128)(2,1)} %bitcast.1676) | data formatting | bytes 6422528 | tf_op jit(solution)/shard_map/all_to_all | solution.py:184
  675.2 6.4 copy.1022
  681.6 45.3 %all_to_all.60 = bf16[49,128,256]{2,0,1:T(8,128)(2,1)S(1)} all-to-all(bf16[49,128,256]{2,0,1:T(8,128)(2,1)} %copy.1022), channel_id=1, replica_groups=mesh['groups'=2,'node'=4,'irrep'=4] {'irrep'}, dimensions={1} | all-to-all | bytes 6422528 | tf_op jit(solution)/shard_map/all_to_all | solution.py:196
  726.9 4.2 copy.1024
  731.1 6.7 dot_general.168
  737.8 5.5 fusion.3
  743.3 6.5 copy.770
  749.8 46.8 %all_to_all.61 = bf16[49,128,256]{2,0,1:T(8,128)(2,1)S(1)} all-to-all(bf16[49,128,256]{2,0,1:T(8,128)(2,1)} %copy.770), channel_id=1, replica_groups=mesh['groups'=2,'node'=4,'irrep'=4] {'irrep'}, dimensions={1} | all-to-all | bytes 6422528 | tf_op jit(solution)/shard_map/all_to_all | solution.py:195
  796.6 4.2 copy.772
  800.8 6.7 dot_general.146
  807.5 3.8 fusion.14
  (1363 shorter events, 457.4 us)
Async XLA Ops:
  7.2 500.5 %copy-start = (bf16[896,896]{1,0:T(8,128)(2,1)S(1)}, bf16[896,896]{1,0:T(8,128)(2,1)}, u32[]{:S(2)}) copy-start(bf16[896,896]{1,0:T(8,128)(2,1)} %param.18) | copy-start | bytes 4816900
  7.2 141.0 %all-gather.2.cloned.1.call-start = ((), (), s32[]{:S(2)}) async-start(), calls=%async_computation.5 | async-start | bytes 2007040 | tf_op jit(solution)/shard_map/all_gather | solution.py:179
  53.3 42.2 %all-to-all-start.2 = ((bf16[4,2,200704]{2,1,0:T(2,128)(2,1)}), bf16[4,2,200704]{2,1,0:T(2,128)(2,1)}, u32[]{:S(2)}, u32[]{:S(2)}) async-start(bf16[4,2,200704]{2,1,0:T(2,128)(2,1)} %reshape.6177), calls=%async_computation.2 | async-start | bytes 6422528 | tf_op jit(solution)/shard_map/all_to_all | solution.py:185
  198.0 121.3 %all-to-all-start = ((bf16[4,2,200704]{2,1,0:T(2,128)(2,1)}), bf16[4,2,200704]{2,1,0:T(2,128)(2,1)}, u32[]{:S(2)}, u32[]{:S(2)}) async-start(bf16[4,2,200704]{2,1,0:T(2,128)(2,1)} %reshape.6175), calls=%async_computation | async-start | bytes 6422528 | tf_op jit(solution)/shard_map/all_to_all | solution.py:184
  203.9 607.5 %reduce-scatter.2.cloned.1.call-start = ((), (), s32[]{:S(2)}) async-start(), calls=%async_computation.6 | async-start | bytes 4014080 | tf_op jit(solution)/shard_map/reduce_scatter | solution.py:206
  252.2 39.7 %copy-start.18 = (f32[1,128,256]{1,2,0:T(8,128)}, f32[1,128,256]{1,2,0:T(8,128)S(1)}, u32[]{:S(2)}) copy-start(f32[1,128,256]{1,2,0:T(8,128)S(1)} %copy.811) | copy-start | bytes 393220
  253.2 38.6 %copy-start.21 = (f32[1,128,256]{1,2,0:T(8,128)}, f32[1,128,256]{1,2,0:T(8,128)S(1)}, u32[]{:S(2)}) copy-start(f32[1,128,256]{1,2,0:T(8,128)S(1)} %copy.823) | copy-start | bytes 393220
  255.6 28.4 %copy-start.372 = (f32[1,256]{1,0:T(1,128)S(1)}, f32[1,256]{1,0:T(1,128)}, u32[]{:S(2)}) copy-start(f32[1,256]{1,0:T(1,128)} %get-tuple-element.328) | copy-start | bytes 3076
  255.6 28.4 %copy-start.374 = (f32[1,256]{1,0:T(1,128)S(1)}, f32[1,256]{1,0:T(1,128)}, u32[]{:S(2)}) copy-start(f32[1,256]{1,0:T(1,128)} %get-tuple-element.332) | copy-start | bytes 3076
  255.6 28.4 %copy-start.380 = (f32[1,256]{1,0:T(1,128)S(1)}, f32[1,256]{1,0:T(1,128)}, u32[]{:S(2)}) copy-start(f32[1,256]{1,0:T(1,128)} %get-tuple-element.329) | copy-start | bytes 3076
  256.3 30.1 %copy-start.12 = (f32[1,128,256]{1,2,0:T(8,128)S(1)}, f32[1,128,256]{1,2,0:T(8,128)}, u32[]{:S(2)}) copy-start(f32[1,128,256]{1,2,0:T(8,128)} %copy.790) | copy-start | bytes 393220
  256.3 30.1 %copy-start.13 = (f32[1,128,256]{1,2,0:T(8,128)S(1)}, f32[1,128,256]{1,2,0:T(8,128)}, u32[]{:S(2)}) copy-start(f32[1,128,256]{1,2,0:T(8,128)} %copy.789) | copy-start | bytes 393220
  256.3 30.1 %copy-start.14 = (f32[1,128,256]{1,2,0:T(8,128)S(1)}, f32[1,128,256]{1,2,0:T(8,128)}, u32[]{:S(2)}) copy-start(f32[1,128,256]{1,2,0:T(8,128)} %copy.788) | copy-start | bytes 393220
  256.3 30.1 %copy-start.15 = (f32[1,128,256]{1,2,0:T(8,128)S(1)}, f32[1,128,256]{1,2,0:T(8,128)}, u32[]{:S(2)}) copy-start(f32[1,128,256]{1,2,0:T(8,128)} %copy.787) | copy-start | bytes 393220
  256.3 30.1 %copy-start.16 = (f32[1,128,256]{1,2,0:T(8,128)S(1)}, f32[1,128,256]{1,2,0:T(8,128)}, u32[]{:S(2)}) copy-start(f32[1,128,256]{1,2,0:T(8,128)} %copy.786) | copy-start | bytes 393220
  256.4 30.1 %copy-start.17 = (f32[1,128,256]{1,2,0:T(8,128)S(1)}, f32[1,128,256]{1,2,0:T(8,128)}, u32[]{:S(2)}) copy-start(f32[1,128,256]{1,2,0:T(8,128)} %copy.785) | copy-start | bytes 393220
  256.4 30.1 %copy-start.332 = (f32[1,256]{1,0:T(1,128)S(1)}, f32[1,256]{1,0:T(1,128)}, u32[]{:S(2)}) copy-start(f32[1,256]{1,0:T(1,128)} %get-tuple-element.293) | copy-start | bytes 3076
  256.4 30.1 %copy-start.338 = (f32[1,256]{1,0:T(1,128)S(1)}, f32[1,256]{1,0:T(1,128)}, u32[]{:S(2)}) copy-start(f32[1,256]{1,0:T(1,128)} %get-tuple-element.294) | copy-start | bytes 3076
  256.4 30.1 %copy-start.344 = (f32[1,256]{1,0:T(1,128)S(1)}, f32[1,256]{1,0:T(1,128)}, u32[]{:S(2)}) copy-start(f32[1,256]{1,0:T(1,128)} %get-tuple-element.295) | copy-start | bytes 3076
  256.4 30.1 %copy-start.352 = (f32[1,256]{1,0:T(1,128)S(1)}, f32[1,256]{1,0:T(1,128)}, u32[]{:S(2)}) copy-start(f32[1,256]{1,0:T(1,128)} %get-tuple-element.296) | copy-start | bytes 3076
  256.4 30.1 %copy-start.358 = (f32[1,256]{1,0:T(1,128)S(1)}, f32[1,256]{1,0:T(1,128)}, u32[]{:S(2)}) copy-start(f32[1,256]{1,0:T(1,128)} %get-tuple-element.297) | copy-start | bytes 3076
  256.4 30.1 %copy-start.364 = (f32[1,256]{1,0:T(1,128)S(1)}, f32[1,256]{1,0:T(1,128)}, u32[]{:S(2)}) copy-start(f32[1,256]{1,0:T(1,128)} %get-tuple-element.298) | copy-start | bytes 3076
  256.4 30.1 %copy-start.368 = (f32[1,256]{1,0:T(1,128)S(1)}, f32[1,256]{1,0:T(1,128)}, u32[]{:S(2)}) copy-start(f32[1,256]{1,0:T(1,128)} %get-tuple-element.292) | copy-start | bytes 3076
  418.1 26.5 %copy-start.174 = (f32[1,128,256]{1,2,0:T(8,128)S(1)}, f32[1,128,256]{1,2,0:T(8,128)}, u32[]{:S(2)}) copy-start(f32[1,128,256]{1,2,0:T(8,128)} %copy.530) | copy-start | bytes 393220
  (495 other events, 4118.4 us)
Sparse Core Ops, SparseCore 0:
  9.6 38.9 all-gather.1
  743.5 62.6 reduce-scatter.1
where the time goes:
time: 832 us; the launch traced here: 818 us
  local copies, waits for them, and re-layouts  421 us (51%)
  other arithmetic  184 us (22%)
  blocking collectives  92.1 us (11%)
  matrix products  65.7 us (8%)
  waiting for transfers between devices  22.3 us (3%)
  between operations  21.8 us (3%)
  starting transfers between devices  11 us (1%)
    unnamed x87, other arithmetic  128 us
    slice x84, local copies, waits for them, and re-layouts, rotate_in(): deg_part[col_index]  119 us
    unnamed x1043, local copies, waits for them, and re-layouts  111 us
    slice x39, local copies, waits for them, and re-layouts, rotate_in(): summed = rot_block[row_index * col_count][None, :] * deg_part[0]  49 us
    all_to_all x1, blocking collectives, local(): lax.all_to_all(sent_edges, 'irrep', split_axis=1, concat_axis=2, tiled=True)  46.8 us
    all_to_all x1, blocking collectives, local(): lax.all_to_all(returned_edges, 'irrep', split_axis=1, concat_axis=2, tile...  45.3 us
    dot_general x18, matrix products, apply_matrix(): return jnp.dot(matrix, operand, preferred_element_type=jnp.float32)  31.8 us
    dot_general x18, matrix products, apply_matrix(): lax.dot_general(matrix, operand, (((0,), (0,)), ((), ())), preferred_elem...  24.6 us
  transfers between devices with their start and end apart: 4, of which 1 were waited for; matrix products, arithmetic and copies ran while one was open for 30% of the time, Pallas kernels for 0%

commit v1 on v0

v1 whole, which is shorter than its diff:
```python
import functools

import jax
import jax.numpy as jnp
from jax import lax
from jax.experimental import pallas as pl
from jax.experimental.pallas import tpu as pltpu
from jax.sharding import PartitionSpec as P

LMAX = 6
MMAX = 2
COEF = (LMAX + 1) ** 2
EDGE_SCALE = 0.5
F32 = jnp.float32
BF16 = jnp.bfloat16
MESH = pl.DeviceIdType.MESH
VMEM_LIMIT = 60 * 1024 * 1024

BASE = [0]
WOFF = [0]
for _l in range(LMAX + 1):
    _rows = 2 * min(_l, MMAX) + 1
    BASE.append(BASE[-1] + _rows)
    WOFF.append(WOFF[-1] + _rows * (2 * _l + 1))
ROWS = BASE[-1]

PARTS = ((0, 4), (4, 6), (6, 7))


def frow(degree, order):
    return BASE[degree] + order + min(degree, MMAX)


def coef_rows(part):
    low, high = PARTS[part]
    return low * low, high * high - low * low


def frame_rows(part):
    low, high = PARTS[part]
    return BASE[low], BASE[high] - BASE[low]


def rotate_in(src, dst, wig, degrees, channels, edges, wig_base):
    halves = channels // 16

    def body(step, carry):
        tile = step // halves
        half = step % halves
        lanes = pl.ds(pl.multiple_of(tile * 128, 128), 128)
        wig_lanes = pl.ds(pl.multiple_of(wig_base + tile * 128, 128), 128)
        chans = pl.ds(pl.multiple_of(half * 16, 16), 16)
        for degree in degrees:
            cols = 2 * degree + 1
            parts = [src[degree * degree + c, chans, lanes].astype(F32) for c in range(cols)]
            for r in range(2 * min(degree, MMAX) + 1):
                at = WOFF[degree] + r * cols
                total = wig[at : at + 1, wig_lanes] * parts[0]
                for c in range(1, cols):
                    total = total + wig[at + c : at + c + 1, wig_lanes] * parts[c]
                dst[BASE[degree] + r, chans, lanes] = total.astype(BF16)
        return carry

    lax.fori_loop(0, (edges // 128) * halves, body, 0)


def rotate_out(src, dst, wig, degrees, channels, edges, wig_base):
    halves = channels // 16

    def body(step, carry):
        tile = step // halves
        half = step % halves
        lanes = pl.ds(pl.multiple_of(tile * 128, 128), 128)
        wig_lanes = pl.ds(pl.multiple_of(wig_base + tile * 128, 128), 128)
        chans = pl.ds(pl.multiple_of(half * 16, 16), 16)
        for degree in degrees:
            cols = 2 * degree + 1
            count = 2 * min(degree, MMAX) + 1
            parts = [src[BASE[degree] + r, chans, lanes].astype(F32) for r in range(count)]
            for c in range(cols):
                at = WOFF[degree] + c
                total = wig[at : at + 1, wig_lanes] * parts[0]
                for r in range(1, count):
                    at = WOFF[degree] + r * cols + c
                    total = total + wig[at : at + 1, wig_lanes] * parts[r]
                dst[degree * degree + c, chans, lanes] = total.astype(BF16)
        return carry

    lax.fori_loop(0, (edges // 128) * halves, body, 0)


def dot_nn(a, b):
    return jnp.dot(a, b, preferred_element_type=F32)


def dot_tn(a, b):
    return lax.dot_general(a, b, (((0,), (0,)), ((), ())), preferred_element_type=F32)


def dot_nt(a, b):
    return lax.dot_general(a, b, (((1,), (1,)), ((), ())), preferred_element_type=F32)


def mix(weights, frame, out, transposed, dtype):
    zero, one, two = weights
    width, share = frame.shape[1], frame.shape[2]
    dot = dot_tn if transposed else dot_nn
    rows = jnp.concatenate([frame[frow(l, 0)] for l in range(LMAX + 1)], axis=0)
    res = dot(zero[...], rows)
    for l in range(LMAX + 1):
        out[frow(l, 0)] = res[l * width : (l + 1) * width].astype(dtype)
    for order, mat in ((1, one), (2, two)):
        degrees = range(order, LMAX + 1)
        rows = jnp.concatenate(
            [
                jnp.concatenate([frame[frow(l, order)], frame[frow(l, -order)]], axis=1)
                for l in degrees
            ],
            axis=0,
        )
        real = dot(mat[0], rows)
        imag = dot(mat[1], rows)
        if transposed:
            plus = real[:, :share] + imag[:, share:]
            minus = real[:, share:] - imag[:, :share]
        else:
            plus = real[:, :share] - imag[:, share:]
            minus = imag[:, :share] + real[:, share:]
        for at, l in enumerate(degrees):
            out[frow(l, order)] = plus[at * width : (at + 1) * width].astype(dtype)
            out[frow(l, -order)] = minus[at * width : (at + 1) * width].astype(dtype)


def kernel(
    n_node,
    n_irrep,
    node_hbm,
    cot_hbm,
    wig_in,
    sources,
    dests,
    fz_hbm,
    fo_hbm,
    ft_hbm,
    sz_hbm,
    so_hbm,
    st_hbm,
    update,
    grad,
    fz,
    fo,
    ft,
    sz,
    so,
    st,
    wig,
    src_table,
    dst_table,
    nodes_all,
    cot_all,
    src_rows,
    seed_rows,
    frame_out,
    frame_in,
    seed_frame,
    hidden,
    back_gate,
    gated,
    message,
    back_hidden,
    back_frame,
    back_in,
    sent_rows,
    ret_rows,
    upd_out,
    upd_in,
    grad_out,
    grad_in,
    load_sem,
    local_sem,
    node_send,
    node_recv,
    cot_send,
    cot_recv,
    fr_send,
    fr_recv,
    bk_send,
    bk_recv,
    up_send,
    up_recv,
    gr_send,
    gr_recv,
):
    group = lax.axis_index("groups")
    me_n = lax.axis_index("node")
    me_i = lax.axis_index("irrep")
    chans, atoms = node_hbm.shape[1], node_hbm.shape[2]
    width = chans * n_irrep
    edges = sources.shape[1]
    share = edges // n_irrep
    all_atoms = atoms * n_node

    def node_peer(k):
        return (group, lax.rem(me_n + k, n_node), me_i)

    def irrep_peer(k):
        return (group, me_n, lax.rem(me_i + k, n_irrep))

    loads = [
        pltpu.make_async_copy(a, b, load_sem.at[i])
        for i, (a, b) in enumerate(
            ((fz_hbm, fz), (fo_hbm, fo), (ft_hbm, ft), (sz_hbm, sz), (so_hbm, so), (st_hbm, st))
        )
    ]

    barrier = pltpu.get_barrier_semaphore()
    for k in range(1, n_node):
        pl.semaphore_signal(barrier, inc=1, device_id=node_peer(k), device_id_type=MESH)
    for k in range(1, n_irrep):
        pl.semaphore_signal(barrier, inc=1, device_id=irrep_peer(k), device_id_type=MESH)
    pl.semaphore_wait(barrier, n_node + n_irrep - 2)

    sends = []

    def remote(src, dst, send, recv, peer):
        copy = pltpu.make_async_remote_copy(
            src_ref=src,
            dst_ref=dst,
            send_sem=send,
            recv_sem=recv,
            device_id=peer,
            device_id_type=MESH,
        )
        copy.start()
        sends.append(copy)
        return copy

    my_atoms = pl.ds(pl.multiple_of(me_n * atoms, atoms), atoms)
    my_chans = pl.ds(pl.multiple_of(me_i * chans, chans), chans)
    my_share = pl.multiple_of(me_i * share, share)
    my_edges = pl.ds(my_share, share)

    node_copies = []
    for part in range(len(PARTS)):
        at, count = coef_rows(part)
        node_copies.append(
            [
                remote(
                    node_hbm.at[pl.ds(at, count)],
                    nodes_all.at[pl.ds(at, count), :, my_atoms],
                    node_send.at[part, k - 1],
                    node_recv.at[part, k - 1],
                    node_peer(k),
                )
                for k in range(1, n_node)
            ]
        )
    cot_copies = [
        remote(
            cot_hbm,
            cot_all.at[:, my_chans, :],
            cot_send.at[k - 1],
            cot_recv.at[k - 1],
            irrep_peer(k),
        )
        for k in range(1, n_irrep)
    ]
    own_node = pltpu.make_async_copy(node_hbm, nodes_all.at[:, :, my_atoms], local_sem.at[0])
    own_cot = pltpu.make_async_copy(cot_hbm, cot_all.at[:, my_chans, :], local_sem.at[1])
    own_node.start()
    own_cot.start()
    for copy in loads:
        copy.start()

    wig[...] = wig_in[...].astype(F32)

    def fill(i, carry):
        at = pl.multiple_of(i * 128, 128)
        rows = lax.broadcasted_iota(jnp.int32, (128, edges), 0) + i * 128
        src_table[pl.ds(at, 128), :] = jnp.where(rows == sources[...], 1.0, 0.0).astype(BF16)
        return carry

    lax.fori_loop(0, all_atoms // 128, fill, 0)
    rows = lax.broadcasted_iota(jnp.int32, (atoms, share), 0)
    dst_table[...] = jnp.where(rows == dests[:, my_edges], 1.0, 0.0).astype(BF16)

    own_cot.wait()
    for copy in cot_copies:
        copy.wait_recv()

    def seed(i, carry):
        cot = cot_all[pl.ds(i * 7, 7)].reshape(7 * width, atoms)
        got = dot_nn(cot, dst_table[...]).astype(BF16)
        seed_rows[pl.ds(i * 7, 7)] = got.reshape(7, width, share)
        return carry

    lax.fori_loop(0, COEF // 7, seed, 0)
    rotate_in(seed_rows, seed_frame, wig, range(LMAX + 1), width, share, my_share)

    own_node.wait()
    frame_copies = []
    own_frames = []
    for part in range(len(PARTS)):
        for copy in node_copies[part]:
            copy.wait_recv()
        at, count = coef_rows(part)

        def gather(i, carry, at=at, count=count):
            lanes = pl.ds(pl.multiple_of(i * 256, 256), 256)
            tab = nodes_all[pl.ds(at, count)].reshape(count * chans, all_atoms)
            got = dot_nn(tab, src_table[:, lanes]).astype(BF16)
            src_rows[pl.ds(at, count), :, lanes] = got.reshape(count, chans, 256)
            return carry

        lax.fori_loop(0, edges // 256, gather, 0)
        rotate_in(src_rows, frame_out, wig, range(*PARTS[part]), chans, edges, 0)
        at, count = frame_rows(part)
        sent = []
        for k in range(1, n_irrep):
            peer = lax.rem(me_i + k, n_irrep)
            lanes = pl.ds(pl.multiple_of(peer * share, share), share)
            sent.append(
                remote(
                    frame_out.at[pl.ds(at, count), :, lanes],
                    frame_in.at[pl.ds(at, count), my_chans, :],
                    fr_send.at[part, k - 1],
                    fr_recv.at[part, k - 1],
                    irrep_peer(k),
                )
            )
        frame_copies.append(sent)
        own = pltpu.make_async_copy(
            frame_out.at[pl.ds(at, count), :, my_edges],
            frame_in.at[pl.ds(at, count), my_chans, :],
            local_sem.at[2 + part],
        )
        own.start()
        own_frames.append(own)

    for copy in loads:
        copy.wait()
    first = (fz, fo, ft)
    second = (sz, so, st)
    mix(second, seed_frame, back_gate, True, F32)
    for part in range(len(PARTS)):
        own_frames[part].wait()
        for copy in frame_copies[part]:
            copy.wait_recv()
    mix(first, frame_in, hidden, False, F32)

    def gate(i, carry):
        rows16 = pl.ds(pl.multiple_of(i * 16, 16), 16)
        s = hidden[0, rows16, :]
        g = jax.nn.sigmoid(s)
        total = jnp.zeros_like(s)
        gated[0, rows16, :] = (s * g).astype(BF16)
        for r in range(1, ROWS):
            h = hidden[r, rows16, :]
            b = back_gate[r, rows16, :]
            total = total + b * h
            gated[r, rows16, :] = (h * g).astype(BF16)
            back_hidden[r, rows16, :] = (b * g).astype(BF16)
        top = back_gate[0, rows16, :] * g * (1.0 + s * (1.0 - g)) + g * (1.0 - g) * total
        back_hidden[0, rows16, :] = top.astype(BF16)
        return carry

    lax.fori_loop(0, width // 16, gate, 0)

    mix(first, back_hidden, back_frame, True, BF16)
    back_copies = []
    own_backs = []
    for part in range(len(PARTS)):
        at, count = frame_rows(part)
        sent = []
        for k in range(1, n_irrep):
            peer = lax.rem(me_i + k, n_irrep)
            theirs = pl.ds(pl.multiple_of(peer * chans, chans), chans)
            sent.append(
                remote(
                    back_frame.at[pl.ds(at, count), theirs, :],
                    back_in.at[pl.ds(at, count), :, my_edges],
                    bk_send.at[part, k - 1],
                    bk_recv.at[part, k - 1],
                    irrep_peer(k),
                )
            )
        back_copies.append(sent)
        own = pltpu.make_async_copy(
            back_frame.at[pl.ds(at, count), my_chans, :],
            back_in.at[pl.ds(at, count), :, my_edges],
            local_sem.at[2 + len(PARTS) + part],
        )
        own.start()
        own_backs.append(own)

    mix(second, gated, message, False, BF16)
    rotate_out(message, sent_rows, wig, range(LMAX + 1), width, share, my_share)

    def aggregate(i, carry):
        rows7 = sent_rows[pl.ds(i * 7, 7)].reshape(7 * width, share)
        got = dot_nt(rows7, dst_table[...]).astype(BF16)
        upd_out[pl.ds(i * 7, 7)] = got.reshape(7, width, atoms)
        return carry

    lax.fori_loop(0, COEF // 7, aggregate, 0)
    upd_copies = []
    for k in range(1, n_irrep):
        peer = lax.rem(me_i + k, n_irrep)
        theirs = pl.ds(pl.multiple_of(peer * chans, chans), chans)
        upd_copies.append(
            remote(
                upd_out.at[:, theirs, :],
                upd_in.at[k - 1],
                up_send.at[k - 1],
                up_recv.at[k - 1],
                irrep_peer(k),
            )
        )

    grad_copies = []
    for part in range(len(PARTS)):
        own_backs[part].wait()
        for copy in back_copies[part]:
            copy.wait_recv()
        rotate_out(back_in, ret_rows, wig, range(*PARTS[part]), chans, edges, 0)
        at, count = coef_rows(part)

        def spread(i, carry, at=at, count=count):
            tab = src_table[pl.ds(pl.multiple_of(i * 2 * atoms, 2 * atoms), 2 * atoms), :]
            got = dot_nt(ret_rows[pl.ds(at, count)].reshape(count * chans, edges), tab)
            got = got.astype(BF16)
            for j in range(2):
                piece = got[:, j * atoms : (j + 1) * atoms].reshape(count, chans, atoms)
                grad_out[2 * i + j, pl.ds(at, count)] = piece
            return carry

        lax.fori_loop(0, n_node // 2, spread, 0)
        sent = []
        for k in range(1, n_node):
            peer = lax.rem(me_n + k, n_node)
            sent.append(
                remote(
                    grad_out.at[peer, pl.ds(at, count)],
                    grad_in.at[k - 1, pl.ds(at, count)],
                    gr_send.at[part, k - 1],
                    gr_recv.at[part, k - 1],
                    node_peer(k),
                )
            )
        grad_copies.append(sent)

    for copy in upd_copies:
        copy.wait_recv()

    def finish_update(i, carry):
        total = upd_out[i, my_chans, :].astype(F32)
        for k in range(n_irrep - 1):
            total = total + upd_in[k, i].astype(F32)
        update[i] = (EDGE_SCALE * total).astype(BF16)
        return carry

    lax.fori_loop(0, COEF, finish_update, 0)

    for part in range(len(PARTS)):
        for copy in grad_copies[part]:
            copy.wait_recv()
        at, count = coef_rows(part)

        def finish_grad(i, carry):
            total = grad_out[me_n, i].astype(F32)
            for k in range(n_node - 1):
                total = total + grad_in[k, i].astype(F32)
            grad[i] = EDGE_SCALE * total
            return carry

        lax.fori_loop(at, at + count, finish_grad, 0)

    for copy in sends:
        copy.wait_send()


def local(
    n_node,
    n_irrep,
    node_feats,
    cotangent,
    wigner,
    sources,
    targets,
    counts,
    first_zero,
    first_one,
    first_two,
    second_zero,
    second_one,
    second_two,
):
    coefs, chans, atoms = node_feats.shape
    edges = sources.shape[0]
    share = edges // n_irrep
    width = chans * n_irrep
    blocks = counts.shape[0]
    slot = jnp.arange(edges // blocks, dtype=jnp.int32)
    live = (slot[None, :] < counts[:, None]).reshape(edges)
    dests = jnp.where(live, targets - lax.axis_index("node") * atoms, -1).reshape(1, edges)
    weights = (first_zero, first_one, first_two, second_zero, second_one, second_two)
    parts = len(PARTS)
    vmem = pltpu.VMEM
    dma = pltpu.SemaphoreType.DMA
    frame = (ROWS, width, share)
    scratch = [vmem(w.shape, BF16) for w in weights] + [
        vmem(wigner.shape, F32),
        vmem((atoms * n_node, edges), BF16),
        vmem((atoms, share), BF16),
        vmem((coefs, chans, atoms * n_node), BF16),
        vmem((coefs, width, atoms), BF16),
        vmem((coefs, chans, edges), BF16),
        vmem((coefs, width, share), BF16),
        vmem((ROWS, chans, edges), BF16),
        vmem(frame, BF16),
        vmem(frame, BF16),
        vmem(frame, F32),
        vmem(frame, F32),
        vmem(frame, BF16),
        vmem(frame, BF16),
        vmem(frame, BF16),
        vmem(frame, BF16),
        vmem((ROWS, chans, edges), BF16),
        vmem((coefs, width, share), BF16),
        vmem((coefs, chans, edges), BF16),
        vmem((coefs, width, atoms), BF16),
        vmem((n_irrep - 1, coefs, chans, atoms), BF16),
        vmem((n_node, coefs, chans, atoms), BF16),
        vmem((n_node - 1, coefs, chans, atoms), BF16),
        dma((len(weights),)),
        dma((2 + 2 * parts,)),
        dma((parts, n_node - 1)),
        dma((parts, n_node - 1)),
        dma((n_irrep - 1,)),
        dma((n_irrep - 1,)),
        dma((parts, n_irrep - 1)),
        dma((parts, n_irrep - 1)),
        dma((parts, n_irrep - 1)),
        dma((parts, n_irrep - 1)),
        dma((n_irrep - 1,)),
        dma((n_irrep - 1,)),
        dma((parts, n_node - 1)),
        dma((parts, n_node - 1)),
    ]
    hbm = pl.BlockSpec(memory_space=pl.ANY)
    inside = pl.BlockSpec(memory_space=pltpu.VMEM)
    return pl.pallas_call(
        functools.partial(kernel, n_node, n_irrep),
        out_shape=(
            jax.ShapeDtypeStruct(node_feats.shape, BF16),
            jax.ShapeDtypeStruct(node_feats.shape, F32),
        ),
        in_specs=[hbm, hbm, inside, inside, inside] + [hbm] * 6,
        out_specs=(inside, inside),
        scratch_shapes=scratch,
        compiler_params=pltpu.CompilerParams(
            collective_id=0, has_side_effects=True, vmem_limit_bytes=VMEM_LIMIT
        ),
        name="edge_conv",
    )(node_feats, cotangent, wigner, sources.reshape(1, edges), dests, *weights)


def solution(mesh):
    node = P(None, "irrep", ("groups", "node"))
    edge = P(("groups", "node"))
    in_specs = (node, node, P(None, ("groups", "node")), edge, edge, edge) + (P(),) * 6
    return jax.shard_map(
        functools.partial(local, mesh.shape["node"], mesh.shape["irrep"]),
        mesh=mesh,
        in_specs=in_specs,
        out_specs=(node, node),
        check_vma=False,
    )
```

time: 832 us -> 110 us (0.13); the launches traced: 818 us -> 109 us
  local copies, waits for them, and re-layouts: 421 us -> 3.85 us
  other arithmetic: 184 us -> 1.35 us
  Pallas kernels: 0 us -> 104 us
  blocking collectives: 92.1 us -> 0 us
  matrix products: 65.7 us -> 0 us
  waiting for transfers between devices: 22.3 us -> 0 us
  between operations: 21.8 us -> 0.64 us
  starting transfers between devices: 11 us -> 0 us
    slice x127 -> x0, local copies, waits for them, and re-layouts: 172 us -> none  [the longest x84 119 us: rotate_in(): deg_part[col_index]]
    unnamed x87 -> x0, other arithmetic: 128 us -> none
    unnamed x1043 -> x2, local copies, waits for them, and re-layouts: 111 us -> 3.85 us
    pallas_call x0 -> x1, Pallas kernels: none -> 104 us  [local(): pl.pallas_call(functools.partial(kernel, n_node, n_irrep), out_shape=(jax...]
    all_to_all x2 -> x0, blocking collectives: 92.1 us -> none  [the longest x1 46.8 us: local(): lax.all_to_all(sent_edges, 'irrep', split_axis=1, concat_axis=2, tiled=True)]
    dot_general x38 -> x0, matrix products: 65.7 us -> none  [the longest x18 31.8 us: apply_matrix(): return jnp.dot(matrix, operand, preferred_element_type=jnp.float32)]
    all_to_all x4 -> x0, local copies, waits for them, and re-layouts: 34.4 us -> none  [the longest x1 13 us: local(): lax.all_to_all(seed_rows, 'irrep', split_axis=2, concat_axis=1, tiled=True)]
    another operation x12 -> x0, local copies, waits for them, and re-layouts: 32.5 us -> none  [the longest x10 19.6 us: rotate_in(): jnp.stack([frame_rows[position] for position in range(len(frame_rows))])]
  transfers between devices with their start and end apart: 4 -> 0, of which waited for: 1 -> 0; matrix products, arithmetic and copies ran while one was open for 30% -> 0% of each run, Pallas kernels for 0% -> 0%
where the time goes in v1:
time: 110 us; the launch traced here: 109 us
  Pallas kernels  104 us (95%)
  local copies, waits for them, and re-layouts  3.85 us (4%)
  other arithmetic  1.35 us (1%)
    pallas_call x1, Pallas kernels, local(): pl.pallas_call(functools.partial(kernel, n_node, n_irrep), out_shape=(jax...  104 us
    unnamed x2, local copies, waits for them, and re-layouts  3.85 us

profile of v1, /device:TPU:1, one launch (start us, length us, event | category | flops | bytes accessed | tf_op | source)
XLA Modules:
  0.0 109.4 jit_solution(5256167098806859263)
XLA Ops:
  0.6 1.4 %subtract_select_fusion = s32[1024]{0:T(1024)} fusion(s32[1024]{0:T(1024)} %param.16, s32[]{:T(128)S(6)} %mul.3, s32[8]{0:T(128)} %param.17), kind=kLoop, calls=%fused_computation | loop fusion | flops 3072 | bytes 8228 | tf_op jit(solution)/shard_map/jit(_where)/select_n | solution.py:505
  2.0 103.5 %edge_conv.1 = (bf16[49,32,128]{2,1,0:T(8,128)(2,1)}, f32[49,32,128]{2,1,0:T(8,128)}) custom-call(bf16[49,32,128]{2,1,0:T(8,128)(2,1)} %node_hbm.1, bf16[49,32,128]{2,1,0:T(8,128)(2,1)} %cot_hbm.1, bf16[235,1024]{1,0:T(8,128)(2,1)} %wig_in.1, s32[1,1024]{1,0:T(1,128)} %bitcast.7, s32[1,1024]{1,0:T(1,128)} %bitcast.6, bf16[896,896]{1,0:T(8,128)(2,1)} %fz_hbm.1, ...), custom_call_target="tpu_custom_call" | custom-call | tf_op jit(solution)/shard_map/edge_conv/pallas_call | solution.py:552
  105.5 1.8 %copy.16 = bf16[49,32,128]{2,1,0:T(8,128)(2,1)} copy(bf16[49,32,128]{2,1,0:T(8,128)(2,1)} %get-tuple-element.4) | data formatting | bytes 802816
  107.3 2.1 %copy.17 = f32[49,32,128]{2,1,0:T(8,128)} copy(f32[49,32,128]{2,1,0:T(8,128)} %get-tuple-element.5) | data formatting | bytes 1605632

commit v2 on v1

--- a/solution.py
+++ b/solution.py
@@ -24,7 +24,9 @@
     WOFF.append(WOFF[-1] + _rows * (2 * _l + 1))
 ROWS = BASE[-1]
 
-PARTS = ((0, 4), (4, 6), (6, 7))
+PARTS = ((6, 7), (5, 6), (4, 5), (0, 3), (3, 4))
+BACK_PARTS = ((0, 1, 2), (4, 3))
+BACK_DEGREES = (range(4, LMAX + 1), range(0, 4))
 
 
 def frow(degree, order):
@@ -101,25 +103,30 @@
     return lax.dot_general(a, b, (((1,), (1,)), ((), ())), preferred_element_type=F32)
 
 
-def mix(weights, frame, out, transposed, dtype):
+def mix(weights, frame, out, transposed, dtype, wanted=range(LMAX + 1)):
     zero, one, two = weights
     width, share = frame.shape[1], frame.shape[2]
     dot = dot_tn if transposed else dot_nn
+
+    def pick(ref, lead, degrees, low):
+        span = pl.ds((degrees[0] - low) * width, len(degrees) * width)
+        return ref[(*lead, slice(None), span) if transposed else (*lead, span, slice(None))]
+
     rows = jnp.concatenate([frame[frow(l, 0)] for l in range(LMAX + 1)], axis=0)
-    res = dot(zero[...], rows)
-    for l in range(LMAX + 1):
-        out[frow(l, 0)] = res[l * width : (l + 1) * width].astype(dtype)
+    res = dot(pick(zero, (), wanted, 0), rows)
+    for at, l in enumerate(wanted):
+        out[frow(l, 0)] = res[at * width : (at + 1) * width].astype(dtype)
     for order, mat in ((1, one), (2, two)):
-        degrees = range(order, LMAX + 1)
+        degrees = [l for l in wanted if l >= order]
         rows = jnp.concatenate(
             [
                 jnp.concatenate([frame[frow(l, order)], frame[frow(l, -order)]], axis=1)
-                for l in degrees
+                for l in range(order, LMAX + 1)
             ],
             axis=0,
         )
-        real = dot(mat[0], rows)
-        imag = dot(mat[1], rows)
+        real = dot(pick(mat, (0,), degrees, order), rows)
+        imag = dot(pick(mat, (1,), degrees, order), rows)
         if transposed:
             plus = real[:, :share] + imag[:, share:]
             minus = real[:, share:] - imag[:, :share]
@@ -166,16 +173,16 @@
     hidden,
     back_gate,
     gated,
-    message,
     back_hidden,
     back_frame,
     back_in,
-    sent_rows,
-    ret_rows,
     upd_out,
+    pair_in,
+    upd_mid,
     upd_in,
     grad_out,
     grad_in,
+    grad_acc,
     load_sem,
     local_sem,
     node_send,
@@ -200,8 +207,26 @@
     share = edges // n_irrep
     all_atoms = atoms * n_node
 
+    n_chip = n_irrep // 2
+    chip, core = me_i // 2, lax.rem(me_i, 2)
+
     def node_peer(k):
         return (group, lax.rem(me_n + k, n_node), me_i)
+
+    def at_node(n):
+        return (group, n, me_i)
+
+    def in_line(n):
+        return jnp.logical_and(n >= 0, n < n_node)
+
+    def chip_of(k):
+        return lax.rem(chip + k, n_chip)
+
+    def chans_of(i):
+        return pl.ds(pl.multiple_of(i * chans, chans), chans)
+
+    def atoms_of(n):
+        return pl.ds(pl.multiple_of(n * atoms, atoms), atoms)
 
     def irrep_peer(k):
         return (group, me_n, lax.rem(me_i + k, n_irrep))
@@ -235,36 +260,54 @@
         sends.append(copy)
         return copy
 
+    line_sends = []
+
+    def line_copy(src, dst, send, recv, peer):
+        return pltpu.make_async_remote_copy(
+            src_ref=src,
+            dst_ref=dst,
+            send_sem=send,
+            recv_sem=recv,
+            device_id=peer,
+            device_id_type=MESH,
+        )
+
+    def line_send(cond, *spec):
+        @pl.when(cond)
+        def _():
+            line_copy(*spec).start()
+
+        line_sends.append((cond, spec))
+
     my_atoms = pl.ds(pl.multiple_of(me_n * atoms, atoms), atoms)
     my_chans = pl.ds(pl.multiple_of(me_i * chans, chans), chans)
     my_share = pl.multiple_of(me_i * share, share)
     my_edges = pl.ds(my_share, share)
 
-    node_copies = []
     for part in range(len(PARTS)):
         at, count = coef_rows(part)
-        node_copies.append(
-            [
-                remote(
+        for dist in (2, 1):
+            for way, sign in ((0, 1), (1, -1)):
+                line_send(
+                    in_line(me_n + sign * dist),
                     node_hbm.at[pl.ds(at, count)],
                     nodes_all.at[pl.ds(at, count), :, my_atoms],
-                    node_send.at[part, k - 1],
-                    node_recv.at[part, k - 1],
-                    node_peer(k),
+                    node_send.at[part, way, dist - 1],
+                    node_recv.at[part, way, dist - 1],
+                    at_node(me_n + sign * dist),
                 )
-                for k in range(1, n_node)
-            ]
-        )
+    beside = (group, me_n, chip * 2 + 1 - core)
+
+    def cot_step(src, hop, k, owner, peer):
+        return remote(
+            src, cot_all.at[:, chans_of(owner), :], cot_send.at[hop, k], cot_recv.at[hop, k], peer
+        )
+
     cot_copies = [
-        remote(
-            cot_hbm,
-            cot_all.at[:, my_chans, :],
-            cot_send.at[k - 1],
-            cot_recv.at[k - 1],
-            irrep_peer(k),
-        )
-        for k in range(1, n_irrep)
+        cot_step(cot_hbm, 0, k, me_i, (group, me_n, chip_of(k) * 2 + core))
+        for k in range(1, n_chip)
     ]
+    cot_near = [cot_step(cot_hbm, 0, 0, me_i, beside)]
     own_node = pltpu.make_async_copy(node_hbm, nodes_all.at[:, :, my_atoms], local_sem.at[0])
     own_cot = pltpu.make_async_copy(cot_hbm, cot_all.at[:, my_chans, :], local_sem.at[1])
     own_node.start()
@@ -285,7 +328,11 @@
     dst_table[...] = jnp.where(rows == dests[:, my_edges], 1.0, 0.0).astype(BF16)
 
     own_cot.wait()
-    for copy in cot_copies:
+    for k, copy in enumerate(cot_copies, 1):
+        copy.wait_recv()
+        owner = chip_of(n_chip - k) * 2 + core
+        cot_near.append(cot_step(cot_all.at[:, chans_of(owner), :], 1, k, owner, beside))
+    for copy in cot_near:
         copy.wait_recv()
 
     def seed(i, carry):
@@ -301,9 +348,30 @@
     frame_copies = []
     own_frames = []
     for part in range(len(PARTS)):
-        for copy in node_copies[part]:
-            copy.wait_recv()
         at, count = coef_rows(part)
+        for dist in (2, 1, *range(3, n_node)):
+            for way, sign in ((0, 1), (1, -1)):
+                here = nodes_all.at[pl.ds(at, count), :, atoms_of(me_n - sign * dist)]
+
+                @pl.when(in_line(me_n - sign * dist))
+                def _(here=here, way=way, sign=sign, dist=dist, part=part):
+                    line_copy(
+                        here,
+                        here,
+                        node_send.at[part, way, dist - 1],
+                        node_recv.at[part, way, dist - 1],
+                        at_node(me_n - sign * dist),
+                    ).wait_recv()
+
+                if 2 <= dist < n_node - 1:
+                    line_send(
+                        jnp.logical_and(in_line(me_n - sign * dist), in_line(me_n + sign)),
+                        here,
+                        here,
+                        node_send.at[part, way, dist],
+                        node_recv.at[part, way, dist],
+                        at_node(me_n + sign),
+                    )
 
         def gather(i, carry, at=at, count=count):
             lanes = pl.ds(pl.multiple_of(i * 256, 256), 256)
@@ -366,34 +434,99 @@
 
     lax.fori_loop(0, width // 16, gate, 0)
 
-    mix(first, back_hidden, back_frame, True, BF16)
-    back_copies = []
-    own_backs = []
-    for part in range(len(PARTS)):
-        at, count = frame_rows(part)
-        sent = []
-        for k in range(1, n_irrep):
-            peer = lax.rem(me_i + k, n_irrep)
-            theirs = pl.ds(pl.multiple_of(peer * chans, chans), chans)
-            sent.append(
+    back_copies = {}
+    own_backs = {}
+    for degrees, parts in zip(BACK_DEGREES, BACK_PARTS):
+        mix(first, back_hidden, back_frame, True, BF16, degrees)
+        for part in parts:
+            at, count = frame_rows(part)
+            back_copies[part] = [
                 remote(
-                    back_frame.at[pl.ds(at, count), theirs, :],
+                    back_frame.at[pl.ds(at, count), chans_of(lax.rem(me_i + k, n_irrep)), :],
                     back_in.at[pl.ds(at, count), :, my_edges],
                     bk_send.at[part, k - 1],
                     bk_recv.at[part, k - 1],
                     irrep_peer(k),
                 )
+                for k in range(1, n_irrep)
+            ]
+            own_backs[part] = pltpu.make_async_copy(
+                back_frame.at[pl.ds(at, count), my_chans, :],
+                back_in.at[pl.ds(at, count), :, my_edges],
+                local_sem.at[2 + len(PARTS) + part],
             )
-        back_copies.append(sent)
-        own = pltpu.make_async_copy(
-            back_frame.at[pl.ds(at, count), my_chans, :],
-            back_in.at[pl.ds(at, count), :, my_edges],
-            local_sem.at[2 + len(PARTS) + part],
-        )
-        own.start()
-        own_backs.append(own)
-
+            own_backs[part].start()
+
+    def grad_spread(part):
+        own_backs[part].wait()
+        for copy in back_copies[part]:
+            copy.wait_recv()
+        rotate_out(back_in, src_rows, wig, range(*PARTS[part]), chans, edges, 0)
+        at, count = coef_rows(part)
+
+        def spread(i, carry, at=at, count=count):
+            tab = src_table[pl.ds(pl.multiple_of(i * 2 * atoms, 2 * atoms), 2 * atoms), :]
+            got = dot_nt(src_rows[pl.ds(at, count)].reshape(count * chans, edges), tab)
+            got = got.astype(BF16)
+            for j in range(2):
+                piece = got[:, j * atoms : (j + 1) * atoms].reshape(count, chans, atoms)
+                grad_out[2 * i + j, pl.ds(at, count)] = piece
+            return carry
+
+        lax.fori_loop(0, n_node // 2, spread, 0)
+
+    def grad_send(part, way, sign, dist, cond):
+        at, count = coef_rows(part)
+        rows = pl.ds(at, count)
+        owner = me_n + sign * dist
+        near = dist <= 2
+        line_send(
+            jnp.logical_and(cond, in_line(owner)),
+            grad_out.at[owner, rows],
+            grad_in.at[way, dist - 1, rows] if near else grad_acc.at[way, dist - 3, rows],
+            gr_send.at[part, way, dist - 1],
+            gr_recv.at[part, way, dist - 1],
+            at_node(owner if near else me_n + sign),
+        )
+
+    def grad_first(part):
+        for dist in range(n_node - 1, 0, -1):
+            for way, sign in ((0, 1), (1, -1)):
+                alone = dist == 1 or dist == n_node - 1
+                grad_send(part, way, sign, dist, True if alone else ~in_line(me_n - sign))
+
+    def grad_later(part):
+        at, count = coef_rows(part)
+        for dist in range(n_node - 2, 1, -1):
+            for way, sign in ((0, 1), (1, -1)):
+                owner = me_n + sign * dist
+                cond = jnp.logical_and(in_line(me_n - sign), in_line(owner))
+                here = grad_acc.at[way, dist - 2, pl.ds(at, count)]
+
+                @pl.when(cond)
+                def _(here=here, way=way, sign=sign, dist=dist, owner=owner):
+                    line_copy(
+                        here,
+                        here,
+                        gr_send.at[part, way, dist],
+                        gr_recv.at[part, way, dist],
+                        at_node(me_n - sign),
+                    ).wait_recv()
+
+                    def add(i, carry):
+                        more = grad_acc[way, dist - 2, i].astype(F32)
+                        grad_out[owner, i] = (grad_out[owner, i].astype(F32) + more).astype(BF16)
+                        return carry
+
+                    lax.fori_loop(at, at + count, add, 0)
+
+                grad_send(part, way, sign, dist, in_line(me_n - sign))
+
+    message, sent_rows = seed_frame, seed_rows
     mix(second, gated, message, False, BF16)
+    order = [part for parts in BACK_PARTS for part in parts]
+    grad_spread(order[0])
+    grad_first(order[0])
     rotate_out(message, sent_rows, wig, range(LMAX + 1), width, share, my_share)
 
     def aggregate(i, carry):
@@ -403,77 +536,94 @@
         return carry
 
     lax.fori_loop(0, COEF // 7, aggregate, 0)
+    pair_copies = [
+        remote(
+            upd_out.at[:, chans_of(chip_of(k) * 2 + 1 - core), :],
+            pair_in.at[k],
+            up_send.at[0, k],
+            up_recv.at[0, k],
+            beside,
+        )
+        for k in range(n_chip)
+    ]
+    grad_later(order[0])
+    grad_spread(order[1])
+    grad_first(order[1])
+    for copy in pair_copies:
+        copy.wait_recv()
     upd_copies = []
-    for k in range(1, n_irrep):
-        peer = lax.rem(me_i + k, n_irrep)
-        theirs = pl.ds(pl.multiple_of(peer * chans, chans), chans)
+    for k in range(1, n_chip):
+
+        def pair_sum(i, carry, k=k):
+            mine = upd_out[i, chans_of(chip_of(k) * 2 + core), :].astype(F32)
+            upd_mid[k - 1, i] = (mine + pair_in[k, i].astype(F32)).astype(BF16)
+            return carry
+
+        lax.fori_loop(0, COEF, pair_sum, 0)
         upd_copies.append(
             remote(
-                upd_out.at[:, theirs, :],
+                upd_mid.at[k - 1],
                 upd_in.at[k - 1],
-                up_send.at[k - 1],
-                up_recv.at[k - 1],
-                irrep_peer(k),
+                up_send.at[1, k],
+                up_recv.at[1, k],
+                (group, me_n, chip_of(k) * 2 + core),
             )
         )
-
-    grad_copies = []
-    for part in range(len(PARTS)):
-        own_backs[part].wait()
-        for copy in back_copies[part]:
-            copy.wait_recv()
-        rotate_out(back_in, ret_rows, wig, range(*PARTS[part]), chans, edges, 0)
-        at, count = coef_rows(part)
-
-        def spread(i, carry, at=at, count=count):
-            tab = src_table[pl.ds(pl.multiple_of(i * 2 * atoms, 2 * atoms), 2 * atoms), :]
-            got = dot_nt(ret_rows[pl.ds(at, count)].reshape(count * chans, edges), tab)
-            got = got.astype(BF16)
-            for j in range(2):
-                piece = got[:, j * atoms : (j + 1) * atoms].reshape(count, chans, atoms)
-                grad_out[2 * i + j, pl.ds(at, count)] = piece
-            return carry
-
-        lax.fori_loop(0, n_node // 2, spread, 0)
-        sent = []
-        for k in range(1, n_node):
-            peer = lax.rem(me_n + k, n_node)
-            sent.append(
-                remote(
-                    grad_out.at[peer, pl.ds(at, count)],
-                    grad_in.at[k - 1, pl.ds(at, count)],
-                    gr_send.at[part, k - 1],
-                    gr_recv.at[part, k - 1],
-                    node_peer(k),
-                )
-            )
-        grad_copies.append(sent)
+    grad_later(order[1])
+    for part in order[2:]:
+        grad_spread(part)
+        grad_first(part)
+        grad_later(part)
 
     for copy in upd_copies:
         copy.wait_recv()
 
     def finish_update(i, carry):
-        total = upd_out[i, my_chans, :].astype(F32)
-        for k in range(n_irrep - 1):
+        total = upd_out[i, my_chans, :].astype(F32) + pair_in[0, i].astype(F32)
+        for k in range(n_chip - 1):
             total = total + upd_in[k, i].astype(F32)
         update[i] = (EDGE_SCALE * total).astype(BF16)
         return carry
 
     lax.fori_loop(0, COEF, finish_update, 0)
 
-    for part in range(len(PARTS)):
-        for copy in grad_copies[part]:
-            copy.wait_recv()
+    for part in order:
         at, count = coef_rows(part)
+        rows = pl.ds(at, count)
+        for way, sign in ((0, 1), (1, -1)):
+            for dist in (1, 2):
+                there = in_line(me_n - sign * dist)
+                here = grad_in.at[way, dist - 1, rows]
+
+                @pl.when(there)
+                def _(here=here, way=way, sign=sign, dist=dist, part=part):
+                    line_copy(
+                        here,
+                        here,
+                        gr_send.at[part, way, dist - 1],
+                        gr_recv.at[part, way, dist - 1],
+                        at_node(me_n - sign * dist),
+                    ).wait_recv()
+
+                @pl.when(jnp.logical_not(there))
+                def _(way=way, dist=dist, rows=rows, count=count):
+                    grad_in[way, dist - 1, rows] = jnp.zeros((count, chans, atoms), BF16)
 
         def finish_grad(i, carry):
             total = grad_out[me_n, i].astype(F32)
-            for k in range(n_node - 1):
-                total = total + grad_in[k, i].astype(F32)
+            for way in range(2):
+                for dist in range(2):
+                    total = total + grad_in[way, dist, i].astype(F32)
             grad[i] = EDGE_SCALE * total
             return carry
 
         lax.fori_loop(at, at + count, finish_grad, 0)
+
+    for cond, spec in line_sends:
+
+        @pl.when(cond)
+        def _(spec=spec):
+            line_copy(*spec).wait_send()
 
     for copy in sends:
         copy.wait_send()
@@ -505,6 +655,7 @@
     dests = jnp.where(live, targets - lax.axis_index("node") * atoms, -1).reshape(1, edges)
     weights = (first_zero, first_one, first_two, second_zero, second_one, second_two)
     parts = len(PARTS)
+    n_chip = n_irrep // 2
     vmem = pltpu.VMEM
     dma = pltpu.SemaphoreType.DMA
     frame = (ROWS, width, share)
@@ -524,28 +675,28 @@
         vmem(frame, BF16),
         vmem(frame, BF16),
         vmem(frame, BF16),
-        vmem(frame, BF16),
         vmem((ROWS, chans, edges), BF16),
-        vmem((coefs, width, share), BF16),
-        vmem((coefs, chans, edges), BF16),
         vmem((coefs, width, atoms), BF16),
-        vmem((n_irrep - 1, coefs, chans, atoms), BF16),
+        vmem((n_chip, coefs, chans, atoms), BF16),
+        vmem((n_chip - 1, coefs, chans, atoms), BF16),
+        vmem((n_chip - 1, coefs, chans, atoms), BF16),
         vmem((n_node, coefs, chans, atoms), BF16),
-        vmem((n_node - 1, coefs, chans, atoms), BF16),
+        vmem((2, 2, coefs, chans, atoms), BF16),
+        vmem((2, n_node - 3, coefs, chans, atoms), BF16),
         dma((len(weights),)),
         dma((2 + 2 * parts,)),
-        dma((parts, n_node - 1)),
-        dma((parts, n_node - 1)),
-        dma((n_irrep - 1,)),
-        dma((n_irrep - 1,)),
+        dma((parts, 2, n_node - 1)),
+        dma((parts, 2, n_node - 1)),
+        dma((2, n_chip)),
+        dma((2, n_chip)),
         dma((parts, n_irrep - 1)),
         dma((parts, n_irrep - 1)),
         dma((parts, n_irrep - 1)),
         dma((parts, n_irrep - 1)),
-        dma((n_irrep - 1,)),
-        dma((n_irrep - 1,)),
-        dma((parts, n_node - 1)),
-        dma((parts, n_node - 1)),
+        dma((2, n_chip)),
+        dma((2, n_chip)),
+        dma((parts, 2, n_node - 1)),
+        dma((parts, 2, n_node - 1)),
     ]
     hbm = pl.BlockSpec(memory_space=pl.ANY)
     inside = pl.BlockSpec(memory_space=pltpu.VMEM)

time: 110 us -> 102 us (0.927)
  Pallas kernels: 104 us -> 95.5 us
    pallas_call x1, Pallas kernels: 104 us -> 95.5 us  [local(): pl.pallas_call(functools.partial(kernel, n_node, n_irrep), out_shape=(jax...]
where the time goes in v2:
time: 102 us; the launch traced here: 101 us
  Pallas kernels  95.5 us (94%)
  local copies, waits for them, and re-layouts  3.85 us (4%)
  other arithmetic  1.35 us (1%)
    pallas_call x1, Pallas kernels, local(): pl.pallas_call(functools.partial(kernel, n_node, n_irrep), out_shape=(jax...  95.5 us
    unnamed x2, local copies, waits for them, and re-layouts  3.85 us

profile of v2, /device:TPU:1, one launch (start us, length us, event | category | flops | bytes accessed | tf_op | source)
XLA Modules:
  0.0 101.4 jit_solution(8291555079053376502)
XLA Ops:
  0.6 1.4 %subtract_select_fusion = s32[1024]{0:T(1024)} fusion(s32[1024]{0:T(1024)} %param.16, s32[]{:T(128)S(6)} %mul.3, s32[8]{0:T(128)} %param.17), kind=kLoop, calls=%fused_computation | loop fusion | flops 3072 | bytes 8228 | tf_op jit(solution)/shard_map/jit(_where)/select_n | solution.py:655
  2.0 95.5 %edge_conv.1 = (bf16[49,32,128]{2,1,0:T(8,128)(2,1)}, f32[49,32,128]{2,1,0:T(8,128)}) custom-call(bf16[49,32,128]{2,1,0:T(8,128)(2,1)} %node_hbm.1, bf16[49,32,128]{2,1,0:T(8,128)(2,1)} %cot_hbm.1, bf16[235,1024]{1,0:T(8,128)(2,1)} %wig_in.1, s32[1,1024]{1,0:T(1,128)} %bitcast.7, s32[1,1024]{1,0:T(1,128)} %bitcast.6, bf16[896,896]{1,0:T(8,128)(2,1)} %fz_hbm.1, ...), custom_call_target="tpu_custom_call" | custom-call | tf_op jit(solution)/shard_map/edge_conv/pallas_call | solution.py:703
  97.5 1.8 %copy.16 = bf16[49,32,128]{2,1,0:T(8,128)(2,1)} copy(bf16[49,32,128]{2,1,0:T(8,128)(2,1)} %get-tuple-element.4) | data formatting | bytes 802816
  99.3 2.1 %copy.17 = f32[49,32,128]{2,1,0:T(8,128)} copy(f32[49,32,128]{2,1,0:T(8,128)} %get-tuple-element.5) | data formatting | bytes 1605632

commit v3 on v2

--- a/solution.py
+++ b/solution.py
@@ -327,23 +327,6 @@
     rows = lax.broadcasted_iota(jnp.int32, (atoms, share), 0)
     dst_table[...] = jnp.where(rows == dests[:, my_edges], 1.0, 0.0).astype(BF16)
 
-    own_cot.wait()
-    for k, copy in enumerate(cot_copies, 1):
-        copy.wait_recv()
-        owner = chip_of(n_chip - k) * 2 + core
-        cot_near.append(cot_step(cot_all.at[:, chans_of(owner), :], 1, k, owner, beside))
-    for copy in cot_near:
-        copy.wait_recv()
-
-    def seed(i, carry):
-        cot = cot_all[pl.ds(i * 7, 7)].reshape(7 * width, atoms)
-        got = dot_nn(cot, dst_table[...]).astype(BF16)
-        seed_rows[pl.ds(i * 7, 7)] = got.reshape(7, width, share)
-        return carry
-
-    lax.fori_loop(0, COEF // 7, seed, 0)
-    rotate_in(seed_rows, seed_frame, wig, range(LMAX + 1), width, share, my_share)
-
     own_node.wait()
     frame_copies = []
     own_frames = []
@@ -404,6 +387,23 @@
         )
         own.start()
         own_frames.append(own)
+
+    own_cot.wait()
+    for k, copy in enumerate(cot_copies, 1):
+        copy.wait_recv()
+        owner = chip_of(n_chip - k) * 2 + core
+        cot_near.append(cot_step(cot_all.at[:, chans_of(owner), :], 1, k, owner, beside))
+    for copy in cot_near:
+        copy.wait_recv()
+
+    def seed(i, carry):
+        cot = cot_all[pl.ds(i * 7, 7)].reshape(7 * width, atoms)
+        got = dot_nn(cot, dst_table[...]).astype(BF16)
+        seed_rows[pl.ds(i * 7, 7)] = got.reshape(7, width, share)
+        return carry
+
+    lax.fori_loop(0, COEF // 7, seed, 0)
+    rotate_in(seed_rows, seed_frame, wig, range(LMAX + 1), width, share, my_share)
 
     for copy in loads:
         copy.wait()

time: 102 us -> 98.7 us (0.968)
  Pallas kernels: 95.5 us -> 92.2 us
    pallas_call x1, Pallas kernels: 95.5 us -> 92.2 us  [local(): pl.pallas_call(functools.partial(kernel, n_node, n_irrep), out_shape=(jax...]
where the time goes in v3:
time: 98.7 us; the launch traced here: 98.1 us
  Pallas kernels  92.2 us (93%)
  local copies, waits for them, and re-layouts  3.85 us (4%)
  other arithmetic  1.35 us (1%)
    pallas_call x1, Pallas kernels, local(): pl.pallas_call(functools.partial(kernel, n_node, n_irrep), out_shape=(jax...  92.2 us
    unnamed x2, local copies, waits for them, and re-layouts  3.85 us

profile of v3, /device:TPU:1, one launch (start us, length us, event | category | flops | bytes accessed | tf_op | source)
XLA Modules:
  0.0 98.1 jit_solution(2051483174648049505)
XLA Ops:
  0.6 1.4 %subtract_select_fusion = s32[1024]{0:T(1024)} fusion(s32[1024]{0:T(1024)} %param.16, s32[]{:T(128)S(6)} %mul.3, s32[8]{0:T(128)} %param.17), kind=kLoop, calls=%fused_computation | loop fusion | flops 3072 | bytes 8228 | tf_op jit(solution)/shard_map/jit(_where)/select_n | solution.py:655
  2.0 92.2 %edge_conv.1 = (bf16[49,32,128]{2,1,0:T(8,128)(2,1)}, f32[49,32,128]{2,1,0:T(8,128)}) custom-call(bf16[49,32,128]{2,1,0:T(8,128)(2,1)} %node_hbm.1, bf16[49,32,128]{2,1,0:T(8,128)(2,1)} %cot_hbm.1, bf16[235,1024]{1,0:T(8,128)(2,1)} %wig_in.1, s32[1,1024]{1,0:T(1,128)} %bitcast.7, s32[1,1024]{1,0:T(1,128)} %bitcast.6, bf16[896,896]{1,0:T(8,128)(2,1)} %fz_hbm.1, ...), custom_call_target="tpu_custom_call" | custom-call | tf_op jit(solution)/shard_map/edge_conv/pallas_call | solution.py:703
  94.2 1.8 %copy.16 = bf16[49,32,128]{2,1,0:T(8,128)(2,1)} copy(bf16[49,32,128]{2,1,0:T(8,128)(2,1)} %get-tuple-element.4) | data formatting | bytes 802816
  96.0 2.1 %copy.17 = f32[49,32,128]{2,1,0:T(8,128)} copy(f32[49,32,128]{2,1,0:T(8,128)} %get-tuple-element.5) | data formatting | bytes 1605632
